TPU v7x, 128 devices: a whole 4x4x4 slice. The times are simulated.
128 devices in a mesh: occ: 8 (over y_hi, x), vir: 16 (over z, y_lo, core).
Axes of the slice: x: 4, y: 4 (y_hi: 2, y_lo: 2; y = y_hi * 2 + y_lo), z: 4, core: 2. Of those that a mesh axis runs over, the one named last changes fastest.
Arguments:
- amplitudes: float32 [4, 32, 128, 128], P(None, 'occ', 'vir'), may hold values from -6 to 6
- vv_factors: float32 [768, 128, 128], P('occ', 'vir'), may hold values from -0.3 to 0.3
- ov_factors: float32 [768, 32, 128], P(None, 'occ', 'vir'), may hold values from -0.3 to 0.3
- occ_irreps: int32 [32], replicated, may hold values from 0 to 7
- vir_irreps: int32 [128], replicated, may hold values from 0 to 7
- aux_irreps: int32 [768], replicated, may hold values from 0 to 7
Outputs:
- residual: float32 [4, 32, 128, 128], P(None, 'occ', 'vir')
Inputs may be any that keep to these rules, and one draw needn't show every extreme that they name: `vir_irreps`: irrep labels of the point group D2h.
All inputs are finite; a program needn't handle non-finite values.
Results may differ from a plain program's by a relative error of at most 0.000086.
Values sent between devices are 32-bit elements; how exact they have to be, the bound alone decides.
No kernel may reach another device: no remote copies, remote signals or barrier semaphores. Data moves between devices by JAX's collectives and lax.ppermute only.
A program may use at most 192 MiB of HBM per device.

v0:
```python
import jax
import jax.numpy as jnp
from jax import lax
from jax.sharding import PartitionSpec as P


def allowed(left, right, target):
    return (jnp.bitwise_xor(left, right) == target).astype(jnp.float32)


def shards(amplitudes, vv_factors, ov_factors, occ_irreps, vir_irreps, aux_irreps):
    high = lax.Precision.HIGHEST
    aux_local = vv_factors.shape[0]
    vir_local = vv_factors.shape[1]
    occ_local = amplitudes.shape[1]
    occ_index = lax.axis_index("occ")
    vir_index = lax.axis_index("vir")
    aux_mine = lax.dynamic_slice_in_dim(aux_irreps, occ_index * aux_local, aux_local)
    vir_mine = lax.dynamic_slice_in_dim(vir_irreps, vir_index * vir_local, vir_local)
    occ_mine = lax.dynamic_slice_in_dim(occ_irreps, occ_index * occ_local, occ_local)
    vv_local = vv_factors * allowed(
        vir_mine[None, :, None], vir_irreps[None, None, :], aux_mine[:, None, None]
    )
    vv_wide = lax.all_gather(vv_factors, "vir", axis=1, tiled=True)
    vv_wide = vv_wide * allowed(
        vir_irreps[None, :, None], vir_irreps[None, None, :], aux_mine[:, None, None]
    )
    pair_all = lax.all_gather(amplitudes, "occ", axis=1, tiled=True)
    inter = jnp.einsum("qac,qbd->acbd", vv_local, vv_wide, precision=high)
    partial_sum = jnp.einsum(
        "ijcd,acbd->ijab",
        lax.all_gather(pair_all, "vir", axis=2, tiled=True),
        inter,
        precision=high,
    )
    ladder = lax.psum_scatter(partial_sum, "occ", scatter_dimension=1, tiled=True)
    swapped = lax.all_to_all(amplitudes, "vir", split_axis=3, concat_axis=2, tiled=True)
    cycle_amps = 2.0 * amplitudes - jnp.transpose(swapped, (0, 1, 3, 2))
    ov_wide = lax.all_gather(ov_factors, "vir", axis=2, tiled=True)
    ov_wide = ov_wide * allowed(
        occ_mine[None, :, None], vir_irreps[None, None, :], aux_irreps[:, None, None]
    )
    factor_part = jnp.einsum("ikac,qkc->iaq", cycle_amps, ov_wide, precision=high)
    factor = lax.psum(factor_part, "occ")
    cycle = jnp.einsum("iaq,qjb->ijab", factor, ov_wide, precision=high)
    return ladder + cycle


def solution(mesh):
    placed = (
        P(None, "occ", "vir", None),
        P("occ", "vir", None),
        P(None, "occ", "vir"),
        P(),
        P(),
        P(),
    )
    return jax.shard_map(
        shards, mesh=mesh, in_specs=placed, out_specs=P(None, "occ", "vir", None), check_vma=False
    )
```

profile of v0, /device:TPU:0, one launch (start us, length us, event | category | flops | bytes accessed | tf_op | source)
XLA Modules:
  0.0 342.9 jit_solution(5576453759396806326)
XLA Ops:
  6.5 0.7 all-gather.8.cloned.1.call-update
  7.3 0.7 all-gather.4.cloned.1.call-update
  8.1 0.8 copy.19
  8.9 35.9 %all_gather.13 = f32[4,32,8,128]{3,2,0,1:T(8,128)S(1)} all-gather(f32[4,4,8,128]{3,2,0,1:T(8,128)S(1)} %copy.19), channel_id=1, replica_groups=mesh['occ'=8,'vir'=16] {'occ'}, dimensions={1}, use_global_device_ids=true | all-gather | bytes 589824 | tf_op jit(solution)/shard_map/all_gather | solution.py:28
  44.8 1.1 copy.20
  45.9 1.4 copy.23
  47.3 1.8 reshape.105
  49.1 5.7 %all-to-all-start = ((f32[16,1,1024]{2,1,0:T(1,128)}), f32[16,1,1024]{2,1,0:T(1,128)S(1)}, u32[]{:S(2)}, u32[]{:S(2)}) async-start(f32[16,1,1024]{2,1,0:T(1,128)} %reshape.105), calls=%async_computation.1 | async-start | bytes 131072 | tf_op jit(solution)/shard_map/all_to_all | solution.py:37
  54.8 0.0 all-reduce.2.cloned.1.call-start
  54.9 0.8 dynamic_slice.10
  55.7 0.7 dynamic_slice.9
  56.4 0.7 dynamic_slice.11
  57.1 0.7 broadcast_xor_fusion.1
  57.8 0.8 broadcast_xor_fusion
  58.7 1.2 select_bitcast_fusion
  59.8 0.7 broadcast_xor_fusion.2
  60.6 0.9 all-to-all-done
  61.5 0.5 broadcast.93
  62.0 0.8 reduce
  62.8 1.2 reshape.106
  64.0 0.6 copy.55
  64.6 0.5 all_to_all.16
  65.2 3.2 fusion.14
  68.4 0.2 reduce-scatter.2.cloned.1.call-start
  68.6 31.9 %all-gather.4.cloned.1.call-done = f32[96,128,128]{2,1,0:T(8,128)} async-done(((f32[96,8,128]{2,1,0:T(8,128)}), f32[96,128,128]{2,1,0:T(8,128)}) %all-gather.4.cloned.1.call-update) | async-done | bytes 6291472 | tf_op jit(solution)/shard_map/all_gather | solution.py:24
  100.5 3.3 compare_select_fusion
  103.8 59.2 %convolution_bitcast_fusion = f32[8,128,128,128,1]{3,1,2,0,4:T(8,128)} fusion(f32[96,128,128]{2,1,0:T(8,128)S(1)} %compare_select_fusion, f32[96,8,128,1]{2,1,0,3:T(8,128)S(1)} %select_bitcast_fusion), kind=kOutput, calls=%fused_computation.2 | convolution fusion | flops 19327352832 | bytes 73793536 | tf_op jit(solution)/shard_map/qac,qbd->acbd/dot_general | solution.py:29
  163.0 98.1 %fusion.9 = f32[4,32,8,128]{3,1,0,2:T(8,128)S(1)} fusion(f32[4,32,128,128]{3,1,2,0:T(8,128)} %all-gather.6.cloned.1.call-done, f32[8,128,128,128,1]{3,1,2,0,4:T(8,128)} %convolution_bitcast_fusion), kind=kOutput, calls=%fused_computation.12 | convolution fusion | flops 25769803776 | bytes 76021760 | tf_op jit(solution)/shard_map/ijcd,acbd->ijab/dot_general | solution.py:30
  261.2 1.1 copy.22
  262.3 70.8 %reduce-scatter.2.cloned.1.call-done = f32[4,4,8,128]{3,2,0,1:T(8,128)} async-done(((f32[4,32,8,128]{3,2,0,1:T(8,128)}), f32[4,4,8,128]{3,2,0,1:T(8,128)}) %reduce-scatter.2.cloned.1.call-update) | async-done | bytes 65552 | tf_op jit(solution)/shard_map/reduce_scatter | solution.py:36
  333.1 2.6 fusion.20
  335.7 0.6 copy.28
  (15 shorter events, 0.2 us)
Async XLA Ops:
  6.5 58.6 %copy-start.1 = (f32[4,4,8,128]{3,2,1,0:T(8,128)S(1)}, f32[4,4,8,128]{3,2,1,0:T(8,128)}, u32[]{:S(2)}) copy-start(f32[4,4,8,128]{3,2,1,0:T(8,128)} %param.6) | copy-start | bytes 196612
  6.5 58.6 %copy-start.2 = (s32[768]{0:T(1024)S(1)}, s32[768]{0:T(1024)}, u32[]{:S(2)}) copy-start(s32[768]{0:T(1024)} %param.11) | copy-start | bytes 9220
  6.5 58.6 %all-gather.8.cloned.1.call-start = ((), (), s32[]{:S(2)}) async-start(), calls=%async_computation.5 | async-start | bytes 1671168 | tf_op jit(solution)/shard_map/all_gather | solution.py:39
  7.3 93.3 %all-gather.4.cloned.1.call-start = ((), (), s32[]{:S(2)}) async-start(), calls=%async_computation.2 | async-start | bytes 6684672 | tf_op jit(solution)/shard_map/all_gather | solution.py:24
  8.0 155.0 %all-gather.6.cloned.1.call-start = ((), (), s32[]{:S(2)}) async-start(), calls=%async_computation.3 | async-start | bytes 8912896 | tf_op jit(solution)/shard_map/all_gather | solution.py:32
  49.1 12.4 %all-to-all-start = ((f32[16,1,1024]{2,1,0:T(1,128)}), f32[16,1,1024]{2,1,0:T(1,128)S(1)}, u32[]{:S(2)}, u32[]{:S(2)}) async-start(f32[16,1,1024]{2,1,0:T(1,128)} %reshape.105), calls=%async_computation.1 | async-start | bytes 131072 | tf_op jit(solution)/shard_map/all_to_all | solution.py:37
  54.8 207.5 %all-reduce.2.cloned.1.call-start = ((), (), s32[]{:S(2)}) async-start(), calls=%async_computation.6 | async-start | bytes 196608 | tf_op jit(solution)/shard_map/psum | solution.py:44
  68.4 264.7 %reduce-scatter.2.cloned.1.call-start = ((), (), s32[]{:S(2)}) async-start(), calls=%async_computation.4 | async-start | bytes 589824 | tf_op jit(solution)/shard_map/reduce_scatter | solution.py:36
  163.0 170.1 %copy-start = (f32[768,4,128]{0,2,1:T(8,128)S(1)}, f32[768,4,128]{0,2,1:T(8,128)}, u32[]{:S(2)}) copy-start(f32[768,4,128]{0,2,1:T(8,128)} %all-gather.8.cloned.1.call-done) | copy-start | bytes 4718596
Sparse Core Ops, SparseCore 0:
  9.0 36.1 all-gather.7
  46.9 53.6 all-gather.3
  102.2 52.1 all-gather.5
  156.8 81.4 all-reduce.1
  262.4 70.6 reduce-scatter.1
where the time goes:
time: 343 us
  matrix products  163 us (48%)
  waiting for transfers between devices  105 us (31%)
  blocking collectives  35.9 us (10%)
  between operations  13.3 us (4%)
  local copies, waits for them, and re-layouts  12 us (3%)
  other arithmetic  7.51 us (2%)
  starting transfers between devices  6.07 us (2%)
    dot_general x1, matrix products, shards(): jnp.einsum('ijcd,acbd->ijab', lax.all_gather(pair_all, 'vir', axis=2, til...  98.1 us
    reduce_scatter x1, waiting for transfers between devices, shards(): lax.psum_scatter(partial_sum, 'occ', scatter_dimension=1, tiled=True)  70.8 us
    dot_general x1, matrix products, shards(): inter = jnp.einsum('qac,qbd->acbd', vv_local, vv_wide, precision=high)  59.2 us
    all_gather x1, blocking collectives, shards(): pair_all = lax.all_gather(amplitudes, 'occ', axis=1, tiled=True)  35.9 us
    all_gather x1, waiting for transfers between devices, shards(): vv_wide = lax.all_gather(vv_factors, 'vir', axis=1, tiled=True)  31.9 us
  transfers between devices with their start and end apart: 6, of which 3 were waited for; matrix products, arithmetic and copies ran while one was open for 52% of the time, Pallas kernels for 0%

commit v1 on v0

--- a/solution.py
+++ b/solution.py
@@ -29,7 +29,9 @@
     inter = jnp.einsum("qac,qbd->acbd", vv_local, vv_wide, precision=high)
     partial_sum = jnp.einsum(
         "ijcd,acbd->ijab",
-        lax.all_gather(pair_all, "vir", axis=2, tiled=True),
+        jnp.concatenate(
+            lax.all_to_all(jnp.stack([pair_all] * lax.axis_size("vir")), "vir", 0, 0), axis=2
+        ),
         inter,
         precision=high,
     )

time: 343 us -> 457 us (1.33)
  waiting for transfers between devices: 105 us -> 198 us
  local copies, waits for them, and re-layouts: 12 us -> 20.9 us
  matrix products: 163 us -> 171 us
  starting transfers between devices: 6.07 us -> 12.6 us
    all_to_all x0 -> x1, waiting for transfers between devices: none -> 128 us  [shards(): lax.all_to_all(jnp.stack([pair_all] * lax.axis_size('vir')), 'vir', 0, 0)]
    all_gather x1, waiting for transfers between devices: 31.9 us -> 0.01 us  [shards(): vv_wide = lax.all_gather(vv_factors, 'vir', axis=1, tiled=True)]
    reshape x0 -> x1, local copies, waits for them, and re-layouts: none -> 8.41 us  [shards(): jnp.concatenate(lax.all_to_all(jnp.stack([pair_all] * lax.axis_size('vir'...]
    dot_general x1, matrix products: 98.1 us -> 106 us  [shards(): jnp.einsum('ijcd,acbd->ijab', jnp.concatenate(lax.all_to_all(jnp.stack([p...]
    all_to_all x0 -> x1, starting transfers between devices: none -> 5.78 us  [shards(): lax.all_to_all(jnp.stack([pair_all] * lax.axis_size('vir')), 'vir', 0, 0)]
  transfers between devices with their start and end apart: 6 -> 6, of which waited for: 3 -> 2; matrix products, arithmetic and copies ran while one was open for 52% -> 42% of each run, Pallas kernels for 0% -> 0%
where the time goes in v1:
time: 457 us
  waiting for transfers between devices  198 us (43%)
  matrix products  171 us (37%)
  blocking collectives  35.4 us (8%)
  local copies, waits for them, and re-layouts  20.9 us (5%)
  between operations  13.3 us (3%)
  starting transfers between devices  12.6 us (3%)
  other arithmetic  4.63 us (1%)
    all_to_all x1, waiting for transfers between devices, shards(): lax.all_to_all(jnp.stack([pair_all] * lax.axis_size('vir')), 'vir', 0, 0)  128 us
    dot_general x1, matrix products, shards(): jnp.einsum('ijcd,acbd->ijab', jnp.concatenate(lax.all_to_all(jnp.stack([p...  106 us
    reduce_scatter x1, waiting for transfers between devices, shards(): lax.psum_scatter(partial_sum, 'occ', scatter_dimension=1, tiled=True)  68.8 us
    dot_general x1, matrix products, shards(): inter = jnp.einsum('qac,qbd->acbd', vv_local, vv_wide, precision=high)  59.3 us
    all_gather x1, blocking collectives, shards(): pair_all = lax.all_gather(amplitudes, 'occ', axis=1, tiled=True)  35.4 us
  transfers between devices with their start and end apart: 6, of which 2 were waited for; matrix products, arithmetic and copies ran while one was open for 42% of the time, Pallas kernels for 0%

profile of v1, /device:TPU:0, one launch (start us, length us, event | category | flops | bytes accessed | tf_op | source)
XLA Modules:
  0.0 456.5 jit_solution(9067215844501986917)
XLA Ops:
  6.5 0.7 all-gather.5.cloned.1.call-update
  7.3 0.7 all-gather.3.cloned.1.call-update
  8.0 1.4 copy.23
  9.4 1.8 reshape.115
  11.2 6.5 %all-to-all-start.1 = ((f32[16,1,1024]{2,1,0:T(1,128)}), f32[16,1,1024]{2,1,0:T(1,128)S(1)}, u32[]{:S(2)}, u32[]{:S(2)}) async-start(f32[16,1,1024]{2,1,0:T(1,128)} %reshape.115), calls=%async_computation.2 | async-start | bytes 131072 | tf_op jit(solution)/shard_map/all_to_all | solution.py:39
  17.7 35.4 %all_gather.10 = f32[4,32,8,128]{3,2,1,0:T(8,128)S(1)} all-gather(f32[4,4,8,128]{3,2,1,0:T(8,128)} %param.6), channel_id=1, replica_groups=mesh['occ'=8,'vir'=16] {'occ'}, dimensions={1}, use_global_device_ids=true | all-gather | bytes 589824 | tf_op jit(solution)/shard_map/all_gather | solution.py:28
  53.2 0.1 copy.19
  53.3 4.3 stack.2
  57.6 5.8 %all-to-all-start = ((f32[16,4,32,8,128]{4,2,3,1,0:T(8,128)}), f32[16,4,32,8,128]{4,2,3,1,0:T(8,128)}, u32[]{:S(2)}, u32[]{:S(2)}) async-start(f32[16,4,32,8,128]{4,2,3,1,0:T(8,128)} %stack.2), calls=%async_computation | async-start | bytes 16777216 | tf_op jit(solution)/shard_map/all_to_all | solution.py:33
  63.5 0.1 dynamic_slice.10
  63.6 0.1 dynamic_slice.9
  63.7 0.1 dynamic_slice.11
  63.7 0.1 broadcast_xor_fusion.2
  63.8 0.1 broadcast_xor_fusion.1
  63.9 0.1 broadcast_xor_fusion
  64.0 0.2 select_bitcast_fusion
  64.1 0.5 broadcast.95
  64.7 0.8 reduce
  65.5 1.2 reshape.116
  66.7 0.6 copy.55
  67.3 0.5 all_to_all.20
  67.9 3.2 fusion.11
  71.1 0.2 reduce-scatter.2.cloned.1.call-start
  71.3 128.0 %all-to-all-done = f32[16,4,32,8,128]{4,2,3,1,0:T(8,128)} async-done(((f32[16,4,32,8,128]{4,2,3,1,0:T(8,128)}), f32[16,4,32,8,128]{4,2,3,1,0:T(8,128)}, u32[]{:S(2)}, u32[]{:S(2)}) %all-to-all-start) | async-done | bytes 8388640 | tf_op jit(solution)/shard_map/all_to_all | solution.py:33
  199.3 8.4 %copy.20 = f32[4,32,16,8,128]{4,1,3,2,0:T(8,128)} copy(f32[4,32,16,8,128]{4,1,3,0,2:T(8,128)} %bitcast.3) | data formatting | bytes 16777216 | tf_op jit(solution)/shard_map/reshape | solution.py:32
  207.7 3.4 compare_select_fusion
  211.2 59.3 %convolution_bitcast_fusion = f32[8,128,128,128,1]{3,1,2,0,4:T(8,128)} fusion(f32[96,128,128]{2,1,0:T(8,128)S(1)} %compare_select_fusion, f32[96,8,128,1]{2,1,0,3:T(8,128)S(1)} %select_bitcast_fusion), kind=kOutput, calls=%fused_computation.2 | convolution fusion | flops 19327352832 | bytes 73793536 | tf_op jit(solution)/shard_map/qac,qbd->acbd/dot_general | solution.py:29
  270.5 106.3 %fusion.8 = f32[4,32,8,128]{3,1,0,2:T(8,128)S(1)} fusion(f32[4,32,128,128,1]{3,1,2,0,4:T(8,128)S(1)} %bitcast.57, f32[8,128,128,128,1]{3,1,2,0,4:T(8,128)} %convolution_bitcast_fusion), kind=kOutput, calls=%fused_computation.11 | convolution fusion | flops 25769803776 | bytes 76021760 | tf_op jit(solution)/shard_map/ijcd,acbd->ijab/dot_general | solution.py:30
  376.7 1.1 copy.22
  377.9 68.8 %reduce-scatter.2.cloned.1.call-done = f32[4,4,8,128]{3,2,0,1:T(8,128)} async-done(((f32[4,32,8,128]{3,2,0,1:T(8,128)}), f32[4,4,8,128]{3,2,0,1:T(8,128)}) %reduce-scatter.2.cloned.1.call-update) | async-done | bytes 65552 | tf_op jit(solution)/shard_map/reduce_scatter | solution.py:38
  446.7 2.6 fusion.17
  449.3 0.6 copy.28
  (26 shorter events, 0.2 us)
Async XLA Ops:
  6.5 61.3 %all-gather.5.cloned.1.call-start = ((), (), s32[]{:S(2)}) async-start(), calls=%async_computation.5 | async-start | bytes 1671168 | tf_op jit(solution)/shard_map/all_gather | solution.py:41
  7.3 200.5 %all-gather.3.cloned.1.call-start = ((), (), s32[]{:S(2)}) async-start(), calls=%async_computation.3 | async-start | bytes 6684672 | tf_op jit(solution)/shard_map/all_gather | solution.py:24
  11.2 42.1 %all-to-all-start.1 = ((f32[16,1,1024]{2,1,0:T(1,128)}), f32[16,1,1024]{2,1,0:T(1,128)S(1)}, u32[]{:S(2)}, u32[]{:S(2)}) async-start(f32[16,1,1024]{2,1,0:T(1,128)} %reshape.115), calls=%async_computation.2 | async-start | bytes 131072 | tf_op jit(solution)/shard_map/all_to_all | solution.py:39
  57.6 5.9 %copy-start.3 = (s32[768]{0:T(1024)S(1)}, s32[768]{0:T(1024)}, u32[]{:S(2)}) copy-start(s32[768]{0:T(1024)} %param.11) | copy-start | bytes 9220
  57.6 6.0 %copy-start.4 = (s32[128]{0:T(128)S(1)}, s32[128]{0:T(128)}, u32[]{:S(2)}) copy-start(s32[128]{0:T(128)} %param.10) | copy-start | bytes 1540
  57.6 6.0 %copy-start.5 = (s32[32]{0:T(128)S(1)}, s32[32]{0:T(128)}, u32[]{:S(2)}) copy-start(s32[32]{0:T(128)} %param.9) | copy-start | bytes 388
  57.6 6.3 %copy-start.1 = (f32[96,8,128]{2,1,0:T(8,128)S(1)}, f32[96,8,128]{2,1,0:T(8,128)}, u32[]{:S(2)}) copy-start(f32[96,8,128]{2,1,0:T(8,128)} %param.7) | copy-start | bytes 1179652
  57.6 10.2 %copy-start.2 = (f32[4,4,8,128]{3,2,1,0:T(8,128)S(1)}, f32[4,4,8,128]{3,2,1,0:T(8,128)}, u32[]{:S(2)}) copy-start(f32[4,4,8,128]{3,2,1,0:T(8,128)} %param.6) | copy-start | bytes 196612
  57.6 141.7 %all-to-all-start = ((f32[16,4,32,8,128]{4,2,3,1,0:T(8,128)}), f32[16,4,32,8,128]{4,2,3,1,0:T(8,128)}, u32[]{:S(2)}, u32[]{:S(2)}) async-start(f32[16,4,32,8,128]{4,2,3,1,0:T(8,128)} %stack.2), calls=%async_computation | async-start | bytes 16777216 | tf_op jit(solution)/shard_map/all_to_all | solution.py:33
  63.4 314.4 %all-reduce.2.cloned.1.call-start = ((), (), s32[]{:S(2)}) async-start(), calls=%async_computation.6 | async-start | bytes 196608 | tf_op jit(solution)/shard_map/psum | solution.py:46
  71.1 375.6 %reduce-scatter.2.cloned.1.call-start = ((), (), s32[]{:S(2)}) async-start(), calls=%async_computation.4 | async-start | bytes 589824 | tf_op jit(solution)/shard_map/reduce_scatter | solution.py:38
  207.7 62.7 %slice-start = ((s8[8388608]{0:T(1024)(128)(4,1)}), s8[4194304]{0:T(1024)(128)(4,1)S(1)}, s32[]{:S(2)}) async-start(s8[8388608]{0:T(1024)(128)(4,1)} %bitcast.55), calls=%async_computation.7 | async-start | bytes 8388608
  211.2 59.3 %slice-start.1 = ((s8[8388608]{0:T(1024)(128)(4,1)}), s8[4194304]{0:T(1024)(128)(4,1)S(1)}, s32[]{:S(2)}) async-start(s8[8388608]{0:T(1024)(128)(4,1)} %bitcast.55), calls=%async_computation.8 | async-start | bytes 8388608
  270.5 176.3 %copy-start = (f32[768,4,128]{0,2,1:T(8,128)S(1)}, f32[768,4,128]{0,2,1:T(8,128)}, u32[]{:S(2)}) copy-start(f32[768,4,128]{0,2,1:T(8,128)} %all-gather.5.cloned.1.call-done) | copy-start | bytes 4718596
Sparse Core Ops, SparseCore 0:
  9.0 36.2 all-gather.4
  46.9 142.9 all-gather.2
  192.4 84.5 all-reduce.1
  378.0 68.6 reduce-scatter.1
